TPU v7x, 32 devices: a whole 2x2x4 slice. The times are simulated.
32 devices in a mesh: dp: 8 (over y, x, core), pipe: 4 (over z).
Axes of the slice: x: 2, y: 2, z: 4, core: 2. Of those that a mesh axis runs over, the one named last changes fastest.
Arguments:
- tokens: bfloat16 [2, 4, 1024, 768], P(None, 'pipe', 'dp'), may hold values from -6 to 6
- lengths: int32 [2, 4, 1], P(None, 'pipe'), may hold values from 960 to 1024, as said below
- cotangent: bfloat16 [2, 4, 1024, 768], P(None, 'pipe', 'dp'), may hold values from -6 to 6
- gain_attn: bfloat16 [768], P('dp'), may hold values from 0.5 to 1.5
- w_query: bfloat16 [768, 768], P('dp'), may hold values from -0.21875 to 0.21875
- w_key: bfloat16 [768, 768], P('dp'), may hold values from -0.21875 to 0.21875
- w_value: bfloat16 [768, 768], P('dp'), may hold values from -0.21875 to 0.21875
- w_out: bfloat16 [768, 768], P('dp'), may hold values from -3 to 3
- gain_mlp: bfloat16 [768], P('dp'), may hold values from 0.5 to 1.5
- w_up: bfloat16 [768, 3072], P('dp'), may hold values from -0.21875 to 0.21875
- w_down: bfloat16 [3072, 768], P('dp'), may hold values from -0.109375 to 0.109375
- pos_bias: bfloat16 [1024, 1024], P('dp'), may hold values from -4 to 4
Outputs:
- output: bfloat16 [2, 4, 1024, 768], P(None, 'pipe', 'dp')
- grad_tokens: bfloat16 [2, 4, 1024, 768], P(None, 'pipe', 'dp')
- grad_gain_attn: float32 [768], P('dp')
- grad_w_query: float32 [768, 768], P('dp')
- grad_w_key: float32 [768, 768], P('dp')
- grad_w_value: float32 [768, 768], P('dp')
- grad_w_out: float32 [768, 768], P('dp')
- grad_gain_mlp: float32 [768], P('dp')
- grad_w_up: float32 [768, 3072], P('dp')
- grad_w_down: float32 [3072, 768], P('dp')
- grad_pos_bias: float32 [1024, 1024], P('dp')
Inputs may be any that keep to these rules, and one draw needn't show every extreme that they name: `lengths`: every sequence has 960 real tokens or more; in every draw some sequence is full and some has exactly that least count.
All inputs are finite; a program needn't handle non-finite values.
Results may differ from a plain program's by a relative error of at most 0.012.
Values may be sent and summed in bfloat16 or wider, within the bound.
A program may use at most 192 MiB of HBM per device.

v0:
```python
import types

import jax
import jax.numpy as jnp
from jax import lax
from jax.experimental import pallas as pl
from jax.experimental.pallas import tpu as pltpu
from jax.sharding import PartitionSpec as P

D = 768
FF = 3072
SEQ = 1024
WIN = 256


EPSILON = 1e-05
GELU_SCALE = 0.7978845608028654
GELU_CUBE = 0.044715
VMEM_BYTES = 63 * 2**20


def normalize(values, gain):
    centre = values - jnp.mean(values, axis=-1, keepdims=True)
    spread = jnp.mean(centre * centre, axis=-1, keepdims=True)
    return centre * lax.rsqrt(spread + EPSILON) * gain


def gelu_tanh(values):
    return jax.nn.gelu(values, approximate=True)


def band_ones(width):
    row_ids = jnp.arange(width)[:, None]
    col_ids = jnp.arange(3 * width)[None, :]
    return (jnp.abs(col_ids - width - row_ids) < width).astype(jnp.float32)


def band_blocks(bias, width):
    length = bias.shape[0]
    padded = jnp.pad(bias, ((0, 0), (width, width)))
    return jnp.stack(
        [
            padded[block * width : (block + 1) * width, block * width : block * width + 3 * width]
            for block in range(length // width)
        ]
    )


def windows(operand, width):
    blocks = operand.shape[0] // width
    padded = jnp.pad(operand, ((width, width), (0, 0))).reshape(blocks + 2, width, operand.shape[1])
    return jnp.concatenate([padded[:-2], padded[1:-1], padded[2:]], axis=1)


def unwindow(grad_windows, width):
    blocks = grad_windows.shape[0]
    leading = jnp.pad(grad_windows[:, :width], ((0, 2), (0, 0), (0, 0)))
    middle = jnp.pad(grad_windows[:, width : 2 * width], ((1, 1), (0, 0), (0, 0)))
    trailing = jnp.pad(grad_windows[:, 2 * width :], ((2, 0), (0, 0), (0, 0)))
    summed = leading + middle + trailing
    return summed[1:-1].reshape(blocks * width, grad_windows.shape[2])


def to_columns(matrix, seq_count, length):
    channels = matrix.shape[1]
    return (
        matrix.reshape(seq_count, length, channels)
        .transpose(1, 0, 2)
        .reshape(length, seq_count * channels)
    )


def from_columns(matrix, seq_count, length):
    channels = matrix.shape[1] // seq_count
    return (
        matrix.reshape(length, seq_count, channels)
        .transpose(1, 0, 2)
        .reshape(seq_count * length, channels)
    )


def outer_sum(left, right):
    return lax.dot_general(
        left, right, (((0,), (0,)), ((), ())), preferred_element_type=jnp.float32
    )


def times_transpose(left, right):
    return lax.dot_general(
        left, right, (((1,), (1,)), ((), ())), preferred_element_type=jnp.float32
    )


def local(
    tokens,
    lengths,
    cotangent,
    gain_attn,
    w_query,
    w_key,
    w_value,
    w_out,
    gain_mlp,
    w_up,
    w_down,
    pos_bias,
):
    gathered = (
        lax.all_gather(gain_attn, "dp", axis=0, tiled=True),
        lax.all_gather(w_query, "dp", axis=0, tiled=True),
        lax.all_gather(w_key, "dp", axis=0, tiled=True),
        lax.all_gather(w_value, "dp", axis=0, tiled=True),
        lax.all_gather(w_out, "dp", axis=0, tiled=True),
        lax.all_gather(gain_mlp, "dp", axis=0, tiled=True),
        lax.all_gather(w_up, "dp", axis=0, tiled=True),
        lax.all_gather(w_down, "dp", axis=0, tiled=True),
        lax.all_gather(pos_bias, "dp", axis=0, tiled=True),
    )
    gain_a = gathered[0].astype(jnp.float32)
    query_w, key_w, value_w, out_w = (gathered[1], gathered[2], gathered[3], gathered[4])
    gain_m = gathered[5].astype(jnp.float32)
    up_w, down_w = (gathered[6], gathered[7])
    bias_full = gathered[8].astype(jnp.float32)
    group_size = lax.axis_size("dp")
    tok_rows = tokens.shape[2]
    seq_count = group_size * tok_rows // SEQ
    band_mask = band_ones(WIN)
    bias_blocks = jnp.exp(band_blocks(bias_full, WIN))
    exp_band = bias_blocks * band_mask
    kernel = ((bias_blocks - 1.0) * band_mask).astype(jnp.bfloat16)
    positions = jnp.arange(SEQ)
    grad_gain_a = jnp.zeros((D,), jnp.float32)
    grad_gain_m = jnp.zeros((D,), jnp.float32)
    grad_query_w = jnp.zeros((D, D), jnp.float32)
    grad_key_w = jnp.zeros((D, D), jnp.float32)
    grad_value_w = jnp.zeros((D, D), jnp.float32)
    grad_out_w = jnp.zeros((D, D), jnp.float32)
    grad_up_w = jnp.zeros((D, FF), jnp.float32)
    grad_down_w = jnp.zeros((FF, D), jnp.float32)
    grad_kernel = jnp.zeros(exp_band.shape, jnp.float32)
    outputs_list = []
    grads_in_list = []
    for micro in range(tokens.shape[0]):
        inputs_f = tokens[micro, 0].astype(jnp.float32)
        normed_f, norm_back_a = jax.vjp(normalize, inputs_f, gain_a)
        normed = normed_f.astype(jnp.bfloat16)
        query = jnp.dot(normed, query_w, preferred_element_type=jnp.float32)
        keys = jnp.dot(normed, key_w, preferred_element_type=jnp.float32).astype(jnp.bfloat16)
        values = jnp.dot(normed, value_w, preferred_element_type=jnp.float32).astype(jnp.bfloat16)
        key_chan, value_chan = (
            lax.all_to_all(keys, "dp", split_axis=1, concat_axis=0, tiled=True),
            lax.all_to_all(values, "dp", split_axis=1, concat_axis=0, tiled=True),
        )
        seq_lengths = lengths[micro, 0]
        channels = key_chan.shape[1]
        valid_seq = (positions[:, None] < seq_lengths[None, :]).astype(jnp.float32)
        valid_cols = jnp.broadcast_to(valid_seq[:, :, None], (SEQ, seq_count, channels)).reshape(
            SEQ, seq_count * channels
        )
        key_cols = to_columns(key_chan, seq_count, SEQ).astype(jnp.float32)
        value_cols = to_columns(value_chan, seq_count, SEQ).astype(jnp.float32)
        weighted = jnp.exp(key_cols) * valid_cols
        col_count = weighted.shape[1]
        operand = jnp.concatenate(
            [(weighted * value_cols).astype(jnp.bfloat16), weighted.astype(jnp.bfloat16)], axis=1
        )
        windowed = windows(operand, WIN)
        banded = jnp.einsum(
            "nqk,nkc->nqc", kernel, windowed, preferred_element_type=jnp.float32
        ).reshape(SEQ, 2 * col_count)
        result = banded + jnp.sum(operand, axis=0, dtype=jnp.float32)[None, :]
        numerator = result[:, :col_count]
        denominator = result[:, col_count:] + 1.0 - valid_cols
        mixed_cols = numerator / denominator * valid_cols
        mixed_tok = lax.all_to_all(
            from_columns(mixed_cols.astype(jnp.bfloat16), seq_count, SEQ),
            "dp",
            split_axis=0,
            concat_axis=1,
            tiled=True,
        )
        sigmoid_q = jax.nn.sigmoid(query)
        mixed_f = mixed_tok.astype(jnp.float32)
        gated = (sigmoid_q * mixed_f).astype(jnp.bfloat16)
        resid = inputs_f + jnp.dot(gated, out_w, preferred_element_type=jnp.float32)
        normed_two_f, norm_back_m = jax.vjp(normalize, resid, gain_m)
        normed_two = normed_two_f.astype(jnp.bfloat16)
        upper = jnp.dot(normed_two, up_w, preferred_element_type=jnp.float32)
        hidden_f, gelu_back = jax.vjp(gelu_tanh, upper)
        hidden = hidden_f.astype(jnp.bfloat16)
        outputs_list.append(
            (resid + jnp.dot(hidden, down_w, preferred_element_type=jnp.float32)).astype(
                jnp.bfloat16
            )
        )
        grad_out = cotangent[micro, 0]
        grad_down_w = grad_down_w + outer_sum(hidden, grad_out)
        grad_hidden = times_transpose(grad_out, down_w)
        grad_upper = gelu_back(grad_hidden)[0].astype(jnp.bfloat16)
        grad_up_w = grad_up_w + outer_sum(normed_two, grad_upper)
        grad_normed_two = times_transpose(grad_upper, up_w)
        grad_resid_norm, grad_gain_part_m = norm_back_m(grad_normed_two)
        grad_gain_m = grad_gain_m + grad_gain_part_m
        grad_resid = grad_out.astype(jnp.float32) + grad_resid_norm
        grad_attn = grad_resid.astype(jnp.bfloat16)
        grad_out_w = grad_out_w + outer_sum(gated, grad_attn)
        grad_gated = times_transpose(grad_attn, out_w)
        grad_mixed = (grad_gated * sigmoid_q).astype(jnp.bfloat16)
        grad_query = (grad_gated * mixed_f * sigmoid_q * (1.0 - sigmoid_q)).astype(jnp.bfloat16)
        grad_mixed_chan = lax.all_to_all(grad_mixed, "dp", split_axis=1, concat_axis=0, tiled=True)
        grad_mixed_cols = to_columns(grad_mixed_chan, seq_count, SEQ).astype(jnp.float32)
        grad_numerator = grad_mixed_cols * valid_cols / denominator
        grad_denominator = -grad_numerator * (numerator / denominator)
        grad_flat = jnp.concatenate(
            [grad_numerator.astype(jnp.bfloat16), grad_denominator.astype(jnp.bfloat16)], axis=1
        )
        grad_result = grad_flat.reshape(SEQ // WIN, WIN, 2 * col_count)
        grad_windowed = jnp.einsum(
            "nqk,nqc->nkc", kernel, grad_result, preferred_element_type=jnp.float32
        )
        grad_kernel = grad_kernel + jnp.einsum(
            "nqc,nkc->nqk", grad_result, windowed, preferred_element_type=jnp.float32
        )
        grad_operand = (
            unwindow(grad_windowed, WIN) + jnp.sum(grad_flat, axis=0, dtype=jnp.float32)[None, :]
        )
        grad_key_value = grad_operand[:, :col_count]
        grad_key_weight = grad_operand[:, col_count:]
        grad_keys_cols = (grad_key_value * value_cols + grad_key_weight) * weighted
        grad_values_cols = grad_key_value * weighted
        grad_keys, grad_values = (
            lax.all_to_all(
                from_columns(grad_keys_cols.astype(jnp.bfloat16), seq_count, SEQ),
                "dp",
                split_axis=0,
                concat_axis=1,
                tiled=True,
            ),
            lax.all_to_all(
                from_columns(grad_values_cols.astype(jnp.bfloat16), seq_count, SEQ),
                "dp",
                split_axis=0,
                concat_axis=1,
                tiled=True,
            ),
        )
        grad_query_w = grad_query_w + outer_sum(normed, grad_query)
        grad_key_w = grad_key_w + outer_sum(normed, grad_keys)
        grad_value_w = grad_value_w + outer_sum(normed, grad_values)
        grad_normed = (
            times_transpose(grad_query, query_w)
            + times_transpose(grad_keys, key_w)
            + times_transpose(grad_values, value_w)
        )
        grad_input_norm, grad_gain_part_a = norm_back_a(grad_normed)
        grad_gain_a = grad_gain_a + grad_gain_part_a
        grads_in_list.append((grad_resid + grad_input_norm).astype(jnp.bfloat16))
    grad_kernel_bias = grad_kernel * exp_band
    grad_bias_pad = jnp.zeros((SEQ, SEQ + 2 * WIN), jnp.float32)
    for block in range(SEQ // WIN):
        grad_bias_pad = grad_bias_pad.at[
            block * WIN : (block + 1) * WIN, block * WIN : block * WIN + 3 * WIN
        ].add(grad_kernel_bias[block])
    grad_bias = grad_bias_pad[:, WIN : WIN + SEQ]
    shares = (
        lax.psum_scatter(grad_gain_a, "dp", scatter_dimension=0, tiled=True),
        lax.psum_scatter(grad_query_w, "dp", scatter_dimension=0, tiled=True),
        lax.psum_scatter(grad_key_w, "dp", scatter_dimension=0, tiled=True),
        lax.psum_scatter(grad_value_w, "dp", scatter_dimension=0, tiled=True),
        lax.psum_scatter(grad_out_w, "dp", scatter_dimension=0, tiled=True),
        lax.psum_scatter(grad_gain_m, "dp", scatter_dimension=0, tiled=True),
        lax.psum_scatter(grad_up_w, "dp", scatter_dimension=0, tiled=True),
        lax.psum_scatter(grad_down_w, "dp", scatter_dimension=0, tiled=True),
        lax.psum_scatter(grad_bias, "dp", scatter_dimension=0, tiled=True),
    )
    reduced = lax.psum(
        (
            shares[0],
            shares[1],
            shares[2],
            shares[3],
            shares[4],
            shares[5],
            shares[6],
            shares[7],
            shares[8],
        ),
        "pipe",
    )
    final_grads = (
        reduced[0],
        reduced[1],
        reduced[2],
        reduced[3],
        reduced[4],
        reduced[5],
        reduced[6],
        reduced[7],
        reduced[8],
    )
    output = jnp.stack(outputs_list)[:, None]
    grad_tokens = jnp.stack(grads_in_list)[:, None]
    return (
        output,
        grad_tokens,
        final_grads[0],
        final_grads[1],
        final_grads[2],
        final_grads[3],
        final_grads[4],
        final_grads[5],
        final_grads[6],
        final_grads[7],
        final_grads[8],
    )


CHIPS = 4
CORES = 2
DEPTH = 4
LANES = 128
TOK = 128
BLK = CORES * TOK
ROWS = D // (CHIPS * CORES)
SL = D // CHIPS
SLP = -(-SL // LANES) * LANES
FS = FF // CHIPS
BAND = 5 * LANES
HALF = D // 2
PACK = ROWS + ROWS // 2
MESH_ID = pl.DeviceIdType.MESH
F32 = jnp.float32
BF = jnp.bfloat16

SCRATCH = dict(
    tok=((BLK, D), BF),
    cot=((SEQ, D), BF),
    gains=((CHIPS * CORES, 16, LANES), BF),
    gain=((16, D), F32),
    wst=((3, ROWS, D), BF),
    wqs=((CHIPS, ROWS, 3 * SLP), BF),
    wqkv=((D, 3 * SLP), BF),
    wout=((CHIPS * SLP, D), BF),
    wup=((D, FS), BF),
    wdn=((FS, D), BF),
    pbw=((TOK, BAND), BF),
    kern=((CHIPS * CORES, TOK, BAND), BF),
    h1=((SEQ, D), BF),
    h2=((SEQ, D), BF),
    n1=((BLK, D), F32),
    r1=((BLK, LANES), F32),
    n2=((BLK, D), F32),
    r2=((BLK, LANES), F32),
    tmp=((HALF, D), F32),
    tmix=((TOK, 2 * SLP), F32),
    sums=((8, 2 * SLP), F32),
    sig=((SEQ, SLP), F32),
    wgt=((SEQ, SLP), F32),
    val=((SEQ, SLP), BF),
    op=((SEQ, 2 * SLP), BF),
    ratio=((SEQ, SLP), F32),
    rden=((SEQ, SLP), F32),
    mixed=((SEQ, SLP), BF),
    gated=((SEQ, SLP), BF),
    grecv=((CHIPS, BLK, SLP), BF),
    ghs=((CHIPS, TOK, LANES), BF),
    ghr=((CHIPS - 1, TOK, LANES), BF),
    gghs=((CHIPS - 1, TOK, LANES), BF),
    gghr=((CHIPS - 1, TOK, LANES), BF),
    resid=((BLK, D), F32),
    hid=((SEQ, FS), BF),
    dge=((3 * BLK, FS), F32),
    gop=((SEQ, 2 * SLP), F32),
    gupr=((SEQ, FS), BF),
    pout=((CHIPS - 1, BLK, D), BF),
    pgh=((CHIPS - 1, BLK, D), BF),
    own=((BLK, D), F32),
    rbout=((6, TOK, D), BF),
    rbg2=((6, TOK, D), BF),
    rbg1=((6, TOK, D), BF),
    gresid=((BLK, D), F32),
    gattn=((BLK, D), BF),
    ggs=((CHIPS - 1, BLK, LANES), BF),
    ggr=((CHIPS, BLK, SLP), BF),
    gdo=((HALF, D), F32),
    gdx=((HALF, D), F32),
    gds=((CHIPS, ROWS, D), BF),
    gdr=((CHIPS, ROWS, D), BF),
    guo=((D, FS), F32),
    gus=((CHIPS, ROWS, FS), BF),
    gur=((CHIPS, ROWS, FS), BF),
    gqo=((CHIPS, ROWS, SLP), F32),
    gqs=((CHIPS, ROWS, SLP), BF),
    gqr=((CHIPS, ROWS, SLP), BF),
    gvo=((CHIPS, ROWS, 2 * SLP), F32),
    gvs=((CHIPS, ROWS, 2 * SLP), BF),
    gvr=((CHIPS, ROWS, 2 * SLP), BF),
    goo=((CHIPS, ROWS, D), F32),
    gos=((CHIPS, ROWS, D), BF),
    gor=((CHIPS, ROWS, D), BF),
    po=((CHIPS - 1, ROWS, D), BF),
    rbo=((6, ROWS // 2, D), BF),
    gko=((CHIPS, TOK, BAND), F32),
    gks=((CHIPS, TOK, BAND), BF),
    gkr=((CHIPS, TOK, BAND), BF),
    pk=((CHIPS - 1, TOK, BAND), BF),
    rbk=((6, TOK // 2, BAND), BF),
    zdb=((CHIPS, ROWS, D), BF),
    zdr=((CHIPS, ROWS, D), BF),
    zdt=((CHIPS, ROWS, D), BF),
    zub=((CHIPS, ROWS, FS), BF),
    zur=((CHIPS, ROWS, FS), BF),
    zut=((CHIPS, ROWS, FS), BF),
    zqb=((CHIPS, PACK, LANES), BF),
    zqr=((CHIPS, PACK, LANES), BF),
    zqt=((CHIPS, PACK, LANES), BF),
    zvb=((CHIPS, 2 * PACK, LANES), BF),
    zvr=((CHIPS, 2 * PACK, LANES), BF),
    zvt=((CHIPS, 2 * PACK, LANES), BF),
    zob=((ROWS, D), BF),
    zor=((ROWS, D), BF),
    zot=((ROWS, D), BF),
    zkb=((TOK, BAND), BF),
    zkr=((TOK, BAND), BF),
    zkt=((TOK, BAND), BF),
    fout=((BLK, D), BF),
    fgt=((BLK, D), BF),
)
POLLS = {
    1: "d3", 2: "d1", 4: "d2 D3", 6: "d0 D1", 9: "D2", 11: "u3", 13: "D0", 15: "u1", 16: "u2 U3", 23: "u0 U1",
    25: "U2", 27: "U0", 28: "q3 q1 q2 q0 o", 29: "Q3 v3 Q1 v1 Q2 v2 Q0 v0 O V3 V1 V2 V0 k", 31: "K",
}
N_REMOTE = 200
N_LOCAL = 40


def dot(left, right, left_dim, right_dim):
    return lax.dot_general(
        left, right, (((left_dim,), (right_dim,)), ((), ())), preferred_element_type=F32
    )


def rows_loop(count, step, body, unroll=1):
    def one(i, carry):
        body(pl.multiple_of(i * step, step))
        return carry

    lax.fori_loop(0, count // step, one, 0, unroll=unroll)


def plane_kernel(
    tok_in, len_in, cot_in, ga_in, gm_in, wq_in, wk_in, wv_in, wout_in, wup_in, wdn_in, pb_in,
    out_out, gtok_out, gq_out, gv_out, gwout_out, gup_out, gdn_out, gpb_out,
    *scratch,
):
    m = types.SimpleNamespace(**dict(zip(SCRATCH, scratch)))
    send_sem, recv_sem, local_sem = scratch[len(SCRATCH):]
    r = lax.axis_index("dp")
    z = lax.axis_index("pipe")
    c = lax.rem(r, 2)
    x = lax.rem(r // 2, 2)
    y = r // 4
    b = r // 2
    length = len_in[c]

    def chip(k):
        return 2 * (1 - y if k // 2 else y) + (1 - x if k % 2 else x)

    def peer(k, other=0):
        return (2 * chip(k) + (1 - c if other else c), z)

    jx, jy, jd = chip(1), chip(2), chip(3)
    SIB, PX, PY, PD = peer(0, 1), peer(1), peer(2), peer(3)
    z_near = z + 1 - 2 * lax.rem(z, 2)
    z_far = 3 - z
    ZN, ZF = (r, z_near), (r, z_far)
    outer = z * (3 - z) == 0
    inner = z * (3 - z) != 0

    remote, locals_ = {}, []
    waited = set()
    begun = []

    def make(name, src, dst, to):
        assert name not in remote, name
        i = len(remote)
        cp = pltpu.make_async_remote_copy(
            src_ref=src, dst_ref=dst, send_sem=send_sem.at[i], recv_sem=recv_sem.at[i],
            device_id=to, device_id_type=MESH_ID,
        )
        remote[name] = cp
        return cp

    def send(name, src, dst, to):
        make(name, src, dst, to)
        start(name)

    def start(*names):
        for name in names:
            begun.append(name)
            remote[name].start()

    def got(*names):
        for name in names:
            if name not in waited:
                waited.add(name)
                remote[name].wait_recv()

    def sent(*names):
        for name in names:
            if name + "/s" not in waited:
                waited.add(name + "/s")
                remote[name].wait_send()

    def local_copy(src, dst):
        cp = pltpu.make_async_copy(src, dst, local_sem.at[len(locals_)])
        locals_.append(cp)
        cp.start()
        return cp

    def ds(start, size, unit):
        return pl.ds(pl.multiple_of(start, unit), size)

    def band_at(d):
        return pl.multiple_of(jnp.minimum(jnp.maximum(d - 2, 0), 3) * LANES, LANES)

    def gather_open(name, blk):
        make(name + "X0", blk(b, 0), blk(b, 0), PX)
        make(name + "Y1", blk(b, 1), blk(b, 1), PY)
        make(name + "X1", blk(b, 1), blk(b, 1), PX)
        make(name + "Y0", blk(b, 0), blk(b, 0), PY)
        make(name + "F0", blk(jx, 0), blk(jx, 0), PY)
        make(name + "F1", blk(jy, 1), blk(jy, 1), PX)

    def gather_start(name):
        start(name + "X0", name + "Y1", name + "X1", name + "Y0")

    def gather_forward(name):
        got(name + "X0")
        start(name + "F0")
        got(name + "Y1")
        start(name + "F1")

    def gather_wait(name, k):
        got(*{1: (name + "X0", name + "X1"), 2: (name + "Y0", name + "Y1"), 3: (name + "F0", name + "F1")}[k])

    fetch = lax.rem(z, 2) == c
    passed = lax.rem(z, 2) != c
    in_fetch = []

    def relay_open(name, place):
        for k in (1, 2, 3):
            make(f"{name}Z{k}", place(k), place(k), ZN)
            in_fetch.append(f"{name}Z{k}")

    def relay(name, place, arrive):
        for k in (1, 2, 3):

            @pl.when(fetch)
            def _(k=k):
                arrive(k)
                start(f"{name}Z{k}")

            @pl.when(passed)
            def _(k=k):
                remote[f"{name}Z{k}"].wait_recv()

            waited.add(f"{name}Z{k}")
            send(f"{name}S{k}", place(k), place(k), SIB)

    def scatter_diagonal(name, part, buf, half):
        send(name + "0", part.at[2, pl.ds(half, half)], buf.at[0], PX)
        send(name + "1", part.at[2, pl.ds(0, half)], buf.at[1], PY)

    def scatter_direct_x(name, part, buf, half):
        send(name + "2", part.at[0, pl.ds(half, half)], buf.at[2], PX)

    def scatter_direct_y(name, part, buf, half):
        send(name + "3", part.at[1, pl.ds(0, half)], buf.at[3], PY)

    def scatter_combine(name, part, buf, half):
        got(name + "1")
        part[0, pl.ds(0, half), :] = (
            part[0, pl.ds(0, half), :].astype(F32) + buf[1].astype(F32)
        ).astype(BF)
        send(name + "4", part.at[0, pl.ds(0, half)], buf.at[4], PX)
        got(name + "0")
        part[1, pl.ds(half, half), :] = (
            part[1, pl.ds(half, half), :].astype(F32) + buf[0].astype(F32)
        ).astype(BF)
        send(name + "5", part.at[1, pl.ds(half, half)], buf.at[5], PY)

    def scatter_wait(name):
        got(name + "2", name + "3", name + "4", name + "5")

    def scatter_sum(buf, half, h, rows):
        if h == 0:
            return buf[3, rows, :].astype(F32) + buf[4, rows, :].astype(F32)
        return buf[2, rows, :].astype(F32) + buf[5, rows, :].astype(F32)

    zitems = {}

    def z_open(name, base, near, total):
        zitems[name] = (
            base,
            near,
            total,
            make(name + "a", base, near, ZN),
            make(name + "b", base, total, ZF),
            make(name + "c", total, total, ZN),
        )

    def z_start(name):
        item = zitems[name]

        @pl.when(outer)
        def _():
            item[3].start()

    def z_mid(name):
        base, near, total, into, across, back = zitems[name]

        @pl.when(inner)
        def _():
            into.wait_recv()
            base[...] = (base[...].astype(F32) + near[...].astype(F32)).astype(BF)
            across.start()

    def z_end(name):
        base, near, total, into, across, back = zitems[name]

        @pl.when(inner)
        def _():
            across.wait_recv()
            total[...] = (base[...].astype(F32) + total[...].astype(F32)).astype(BF)
            back.start()

        @pl.when(outer)
        def _():
            back.wait_recv()

    def z_close(name):
        base, near, total, into, across, back = zitems[name]

        @pl.when(outer)
        def _():
            into.wait_send()

        @pl.when(inner)
        def _():
            across.wait_send()
            back.wait_send()

    for k in range(CHIPS):
        j = chip(k)
        z_open(f"zd{k}", m.zdb.at[j], m.zdr.at[j], m.zdt.at[j])
        z_open(f"zu{k}", m.zub.at[j], m.zur.at[j], m.zut.at[j])
        z_open(f"zq{k}", m.zqb.at[j], m.zqr.at[j], m.zqt.at[j])
        z_open(f"zv{k}", m.zvb.at[j], m.zvr.at[j], m.zvt.at[j])
    z_open("zo", m.zob, m.zor, m.zot)
    z_open("zk", m.zkb, m.zkr, m.zkt)
    ORDER = (3, 1, 2, 0)

    def spread(name, k, total, landing):
        if k:
            send(f"{name}{k}", total.at[chip(k)], landing.at[b], peer(k))
        else:
            local_copy(total.at[b], landing.at[b])

    def poll(place):
        for step in POLLS.get(place, "").split():
            name = "z" + step.lower()
            if step.islower():
                z_mid(name)
                continue
            z_end(name)
            which, k = step[0], chip(int(step[1:] or 0))
            if which == "D":
                local_copy(m.zdt.at[k], gdn_out.at[k])
            elif which == "U":
                spread("fu", int(step[1]), m.zut, gup_out)
            elif which == "Q":
                spread("fq", int(step[1]), m.zqt, gq_out)
            elif which == "V":
                spread("fv", int(step[1]), m.zvt, gv_out)
            elif which == "O":
                local_copy(m.zot, gwout_out)
            else:
                local_copy(m.zkt, gpb_out)

    own_half = ds(c * TOK, TOK, TOK)
    other_half = ds((1 - c) * TOK, TOK, TOK)
    l_tok = local_copy(tok_in.at[c], m.tok.at[own_half])
    l_w = [local_copy(w, m.wst.at[i]) for i, w in enumerate((wq_in, wk_in, wv_in))]
    l_pb = local_copy(pb_in.at[:, ds(band_at(r), BAND, LANES)], m.pbw)

    def wout_rows(j, core):
        return m.wout.at[ds(j * SLP + core * ROWS, ROWS, 32)]

    l_wout = local_copy(wout_in, wout_rows(b, c))
    up_rows = ds(r * ROWS, ROWS, 32)
    l_wup = local_copy(wup_in.at[:, ds(b * FS, FS, LANES)], m.wup.at[up_rows])
    dn_rows = ds(c * HALF, HALF, LANES)
    l_wdn = local_copy(wdn_in, m.wdn.at[dn_rows])
    cot_half = ds(b * BLK + c * TOK, TOK, TOK)
    l_cot = local_copy(cot_in.at[c], m.cot.at[cot_half])

    line = lax.broadcasted_iota(jnp.int32, (16, LANES), 0)
    fill = jnp.zeros((1, LANES - ROWS), F32)
    both_gains = [
        jnp.broadcast_to(jnp.concatenate([g[...].astype(F32), fill], axis=1), (16, LANES)) for g in (ga_in, gm_in)
    ]
    m.gains[r] = jnp.where(line == 0, both_gains[0], both_gains[1]).astype(BF)

    barrier = pltpu.get_barrier_semaphore()
    everyone = [peer(k, o) for k in range(CHIPS) for o in range(CORES) if (k, o) != (0, 0)] + [ZN, ZF]
    for other in everyone:
        pl.semaphore_signal(barrier, inc=1, device_id=other, device_id_type=MESH_ID)
    l_pb.wait()
    t_ids = r * TOK + lax.broadcasted_iota(jnp.int32, (TOK, BAND), 0)
    u_ids = band_at(r) + lax.broadcasted_iota(jnp.int32, (TOK, BAND), 1)
    in_band = jnp.abs(t_ids - u_ids) < WIN
    m.kern[r] = jnp.where(in_band, jnp.exp(m.pbw[...].astype(F32)) - 1.0, 0.0).astype(BF)

    for cp in l_w:
        cp.wait()
    for i in range(3):
        w_rows = m.wst[i].astype(F32)
        for j in range(CHIPS):
            piece = w_rows[:, j * SL : (j + 1) * SL]
            m.wqs[j, :, i * SLP : (i + 1) * SLP] = jnp.concatenate(
                [piece, jnp.zeros((ROWS, SLP - SL), F32)], axis=1
            ).astype(BF)
    pl.semaphore_wait(barrier, len(everyone))

    send("tokS", tok_in.at[1 - c], m.tok.at[own_half], SIB)
    gain_names = []
    for k in range(CHIPS):
        for o in range(CORES):
            if (k, o) != (0, 0):
                gain_names.append(f"gain{k}{o}")
                send(gain_names[-1], m.gains.at[r], m.gains.at[r], peer(k, o))

    def wout_blk(j, h):
        return m.wout.at[ds(j * SLP + c * ROWS + h * (ROWS // 2), ROWS // 2, 16)]

    gather_open("wo", wout_blk)
    in_fetch.extend("wo" + part for part in ("X0", "X1", "Y0", "Y1", "F0", "F1"))
    l_wout.wait()

    @pl.when(fetch)
    def _():
        gather_start("wo")

    for k, to in ((1, PX), (2, PY), (3, PD)):
        make(f"wq{k}", m.wqs.at[chip(k)], m.wqkv.at[up_rows], to)
        in_fetch.append(f"wq{k}")

    @pl.when(fetch)
    def _():
        start("wq1", "wq2", "wq3")

    def kern_blk(j, h):
        return m.kern.at[2 * j + c, pl.ds(h * (TOK // 2), TOK // 2)]

    gather_open("kn", kern_blk)
    in_fetch.extend("kn" + part for part in ("X0", "X1", "Y0", "Y1", "F0", "F1"))

    @pl.when(fetch)
    def _():
        gather_start("kn")

    send("knS0", m.kern.at[r], m.kern.at[r], SIB)

    send("wqS0", m.wqs.at[b], m.wqkv.at[up_rows], SIB)
    m.wqkv[up_rows, :] = m.wqs[b]

    def norm(src, n_ref, r_ref):
        def body(i):
            rows = pl.ds(i, 32)
            values = src[rows, :].astype(F32)
            centre = values - jnp.mean(values, axis=-1, keepdims=True)
            spread = jnp.mean(centre * centre, axis=-1, keepdims=True)
            rinv = lax.rsqrt(spread + EPSILON)
            n_ref[rows, :] = centre * rinv
            r_ref[rows, :] = jnp.broadcast_to(rinv, (32, LANES))

        rows_loop(BLK, 32, body, unroll=2)

    def scale(n_ref, gain_row, dst, base):
        def body(i):
            dst[pl.ds(pl.multiple_of(base + i, 32), 32), :] = (
                n_ref[pl.ds(i, 32), :] * m.gain[gain_row : gain_row + 1, :]
            ).astype(BF)

        rows_loop(BLK, 32, body, unroll=2)

    l_tok.wait()
    got("tokS")
    norm(m.tok, m.n1, m.r1)
    got(*gain_names)
    m.gain[...] = jnp.concatenate(
        [m.gains[d].astype(F32)[:, :ROWS] for d in range(CHIPS * CORES)], axis=1
    )
    scale(m.n1, 0, m.h1, b * BLK)

    def h1_blk(j, h):
        return m.h1.at[ds(j * BLK + h * TOK, TOK, TOK)]

    gather_open("h1", h1_blk)
    gather_start("h1")

    def w_place(ref):
        return lambda k: ref.at[ds((2 * chip(k) + c) * ROWS, ROWS, 32)]

    wq_place = w_place(m.wqkv)
    relay_open("wq", wq_place)
    relay("wq", wq_place, lambda k: got(f"wq{k}"))

    @pl.when(fetch)
    def _():
        gather_forward("kn")

    gather_forward("h1")
    for j in range(CHIPS):
        m.wout[j * SLP + SL : (j + 1) * SLP, :] = jnp.zeros((SLP - SL, D), BF)

    for k, to in ((1, PX), (2, PY), (3, PD)):
        make(f"wu{k}", wup_in.at[:, ds(chip(k) * FS, FS, LANES)], m.wup.at[up_rows], to)
        in_fetch.append(f"wu{k}")

    @pl.when(fetch)
    def _():
        gather_forward("wo")
        start("wu1", "wu2", "wu3")

    send("woS0", wout_rows(b, c), wout_rows(b, c), SIB)
    l_wup.wait()
    send("wuS0", m.wup.at[up_rows], m.wup.at[up_rows], SIB)
    l_wdn.wait()
    send("wdS", m.wdn.at[dn_rows], m.wdn.at[dn_rows], SIB)
    send("cotS", cot_in.at[1 - c], m.cot.at[cot_half], SIB)
    got("wqS0", "wqS1", "wqS2", "wqS3")

    def blk_rows(j):
        return ds(j * BLK, BLK, BLK)

    def project(j):
        m.tmp[0:BLK, :] = dot(m.h1[blk_rows(j), :], m.wqkv[...], 1, 0)

        def body(i):
            rows = pl.ds(i, 16)
            at = pl.multiple_of(j * BLK + i, 16)
            to = pl.ds(at, 16)
            q = m.tmp[rows, 0:SLP]
            m.sig[to, :] = 1.0 / (1.0 + jnp.exp(-q))
            keys = m.tmp[rows, SLP : 2 * SLP].astype(BF).astype(F32)
            values = m.tmp[rows, 2 * SLP : 3 * SLP].astype(BF)
            pos = at + lax.broadcasted_iota(jnp.int32, (16, SLP), 0)
            weighted = jnp.where(pos < length, jnp.exp(keys), 0.0)
            m.wgt[to, :] = weighted
            m.val[to, :] = values
            m.op[to, 0:SLP] = (weighted * values.astype(F32)).astype(BF)
            m.op[to, SLP : 2 * SLP] = weighted.astype(BF)

        rows_loop(BLK, 16, body, unroll=2)

    project(b)
    kn_place = lambda k: m.kern.at[2 * chip(k) + c]
    relay_open("kn", kn_place)
    relay("kn", kn_place, lambda k: gather_wait("kn", k))
    for k in (1, 2):
        gather_wait("h1", k)
        project(chip(k))
    gather_wait("h1", 3)
    project(jd)
    l_cot.wait()
    got("cotS")

    def cot_blk(j, h):
        return m.cot.at[ds(j * BLK + h * TOK, TOK, TOK)]

    gather_open("ct", cot_blk)
    start("ctX0", "ctY1")

    got("knS0", "knS1", "knS2", "knS3")
    ones = jnp.ones((8, SEQ), BF)
    m.sums[...] = dot(ones, m.op[...], 1, 0)

    def mix(j, half):
        d = 2 * j + half
        m.tmix[...] = dot(m.kern[d], m.op[pl.ds(band_at(d), BAND), :], 1, 0)

        def body(i):
            rows = pl.ds(i, 32)
            at = pl.multiple_of(d * TOK + i, 32)
            to = pl.ds(at, 32)
            pos = at + lax.broadcasted_iota(jnp.int32, (32, SLP), 0)
            valid = jnp.where(pos < length, 1.0, 0.0)
            num = m.tmix[rows, 0:SLP] + m.sums[0:1, 0:SLP]
            den = m.tmix[rows, SLP : 2 * SLP] + m.sums[0:1, SLP : 2 * SLP] + 1.0 - valid
            rden = 1.0 / den
            ratio = num * rden
            mixed = (ratio * valid).astype(BF)
            m.ratio[to, :] = ratio
            m.rden[to, :] = rden * valid
            m.mixed[to, :] = mixed
            gated = m.sig[to, :] * mixed.astype(F32)
            m.gated[to, :] = gated.astype(BF)
            high = gated[:, LANES:]
            m.ghs[j, rows, :] = jnp.where(
                half == 0, high, m.ghs[j, rows, :].astype(F32) + pltpu.roll(high, SL - LANES, 1)
            ).astype(BF)

        rows_loop(TOK, 32, body, unroll=2)

    def mix_block(j):
        def one(i, carry):
            mix(j, i)
            return carry

        lax.fori_loop(0, CORES, one, 0)

    low_lanes = pl.ds(0, LANES)

    def unpack(dst, high):
        lane = lax.broadcasted_iota(jnp.int32, (TOK, LANES), 1)
        both = high[...].astype(F32)
        for h in range(2):
            part = both if h == 0 else pltpu.roll(both, LANES - (SL - LANES), 1)
            dst[h * TOK : (h + 1) * TOK, LANES:] = jnp.where(lane < SL - LANES, part, 0.0).astype(BF)

    for k, to in ((3, PD), (1, PX), (2, PY)):
        j = chip(k)
        mix_block(j)
        send(f"ga{k}", m.gated.at[blk_rows(j), low_lanes], m.grecv.at[k, :, low_lanes], to)
        send(f"gh{k}", m.ghs.at[j], m.ghr.at[k - 1], to)
    mix_block(b)
    m.grecv[0] = m.gated[blk_rows(b), :]

    gather_forward("ct")
    wo_place = lambda k: wout_rows(chip(k), c)
    relay_open("wo", wo_place)
    relay("wo", wo_place, lambda k: gather_wait("wo", k))
    wu_place = w_place(m.wup)
    relay_open("wu", wu_place)
    relay("wu", wu_place, lambda k: got(f"wu{k}"))

    got("woS0", "woS1", "woS2", "woS3")
    m.resid[...] = m.tok[...].astype(F32)
    for k in (0, 1, 2, 3):
        if k:
            got(f"ga{k}", f"gh{k}")
            unpack(m.grecv.at[k], m.ghr.at[k - 1])
        m.resid[...] += dot(m.grecv[k], m.wout[ds(chip(k) * SLP, SLP, SLP), :], 1, 0)
    norm(m.resid, m.n2, m.r2)
    scale(m.n2, 1, m.h2, b * BLK)

    def h2_blk(j, h):
        return m.h2.at[ds(j * BLK + h * TOK, TOK, TOK)]

    gather_open("h2", h2_blk)
    gather_start("h2")

    got("wuS0", "wuS1", "wuS2", "wuS3", "wdS")

    def ff_forward(k):
        j = chip(k)
        keep = (k % 3) * BLK
        m.tmp[0:BLK, :] = dot(m.h2[blk_rows(j), :], m.wup[...], 1, 0)

        def gelu(i):
            v = m.tmp[pl.ds(i, 16), :]
            square = v * v
            t = jnp.tanh(GELU_SCALE * v * (1.0 + GELU_CUBE * square))
            half = 0.5 * (1.0 + t)
            m.hid[pl.ds(pl.multiple_of(j * BLK + i, 16), 16), :] = (v * half).astype(BF)
            m.dge[pl.ds(pl.multiple_of(keep + i, 16), 16), :] = half + 0.5 * v * (1.0 - t * t) * (
                GELU_SCALE * (1.0 + 3.0 * GELU_CUBE * square)
            )

        rows_loop(BLK, 16, gelu, unroll=2)

    def ff_out(k):
        part = dot(m.hid[blk_rows(chip(k)), :], m.wdn[...], 1, 0)
        if k == 0:
            m.resid[...] += part
        else:
            m.pout[k - 1] = part.astype(BF)

    def ff_backward(k):
        j = chip(k)
        keep = (k % 3) * BLK
        m.tmp[0:BLK, :] = dot(m.cot[blk_rows(j), :], m.wdn[...], 1, 1)

        def back(i):
            m.gupr[pl.ds(pl.multiple_of(j * BLK + i, 16), 16), :] = (
                m.tmp[pl.ds(i, 16), :] * m.dge[pl.ds(pl.multiple_of(keep + i, 16), 16), :]
            ).astype(BF)

        rows_loop(BLK, 16, back, unroll=2)
        part = dot(m.gupr[blk_rows(j), :], m.wup[...], 1, 1)
        if k == 0:
            m.own[...] = part
        else:
            m.pgh[k - 1] = part.astype(BF)

    other_cols = ds((1 - c) * HALF, HALF, LANES)
    own_cols = ds(c * HALF, HALF, LANES)

    def ff_grads(k):
        rows = blk_rows(chip(k))
        for dst, at, left, cols, right in (
            (m.gdx, 0, m.hid, other_cols, m.cot),
            (m.gdo, 0, m.hid, own_cols, m.cot),
            (m.guo, 0, m.h2, pl.ds(0, HALF), m.gupr),
            (m.guo, HALF, m.h2, pl.ds(HALF, HALF), m.gupr),
        ):
            part = dot(left[rows, cols], right[rows, :], 0, 0)
            to = pl.ds(at, HALF)
            if k == 0:
                dst[to, :] = part
            else:
                dst[to, :] += part

    ff_forward(0)
    ff_backward(0)
    gather_forward("h2")
    start("ctX1", "ctY0")
    ff_out(0)
    ff_grads(0)
    for k in (1, 2):
        gather_wait("h2", k)
        ff_forward(k)
    gather_wait("h2", 3)
    ff_forward(3)
    gather_wait("ct", 3)
    ff_backward(3)
    scatter_diagonal("g2", m.pgh, m.rbg2, TOK)
    gather_wait("ct", 1)
    ff_backward(1)
    scatter_direct_x("g2", m.pgh, m.rbg2, TOK)
    gather_wait("ct", 2)
    ff_backward(2)
    scatter_direct_y("g2", m.pgh, m.rbg2, TOK)
    ff_grads(3)
    ff_grads(1)
    scatter_combine("g2", m.pgh, m.rbg2, TOK)
    ff_grads(2)

    for j in range(CHIPS):
        m.gds[j] = m.gdx[j * ROWS : (j + 1) * ROWS, :].astype(BF)
    send("gdS", m.gds, m.gdr, SIB)
    for j in range(CHIPS):
        m.gus[j] = m.guo[ds((2 * j + 1 - c) * ROWS, ROWS, 32), :].astype(BF)
    send("guS", m.gus, m.gur, SIB)

    def split_rows(left, right, kept, leaving):
        width = right.shape[1]
        for i in range(2):
            m.tmp[:, 0:width] = dot(left[:, i * HALF : (i + 1) * HALF], right[...], 0, 0)
            for q in range(2):
                kept[2 * i + q] = m.tmp[ds((2 * q + c) * ROWS, ROWS, 32), 0:width]
                leaving[2 * i + q] = m.tmp[ds((2 * q + 1 - c) * ROWS, ROWS, 32), 0:width].astype(BF)

    def pair_sum(name, kept, came, base):
        for k in ORDER:
            j = chip(k)
            base[j] = (kept(j) + came[j].astype(F32)).astype(BF)
            z_start(f"{name}{k}")

    def pack(dst, at, rows):
        n = rows.shape[0]
        dst[at : at + n, :] = rows[:, :LANES].astype(BF)
        dst[at + n : at + n + n // 2, :] = jnp.concatenate(
            [rows[: n // 2, LANES:SL], rows[n // 2 :, LANES:SL]], axis=1
        ).astype(BF)

    def pair_sum_packed(name, kept, came, base):
        for k in ORDER:
            j = chip(k)
            total = kept[j] + came[j].astype(F32)
            for i in range(total.shape[1] // SLP):
                pack(base.at[j], i * PACK, total[:, i * SLP : (i + 1) * SLP])
            z_start(f"{name}{k}")

    got("gdS")
    pair_sum("zd", lambda j: m.gdo[ds(j * ROWS, ROWS, 32), :], m.gdr, m.zdb)
    got("guS")
    pair_sum("zu", lambda j: m.guo[ds((2 * j + c) * ROWS, ROWS, 32), :], m.gur, m.zub)
    for k in (3, 1, 2):
        ff_out(k)
    scatter_diagonal("ou", m.pout, m.rbout, TOK)
    poll(1)

    scatter_wait("g2")

    def norm_back(total, gain_row, n_ref, r_ref, i, base):
        rows = pl.ds(i, 32)
        e = total * m.gain[gain_row : gain_row + 1, :]
        n = n_ref[rows, :]
        mean_e = jnp.mean(e, axis=-1, keepdims=True)
        mean_en = jnp.mean(e * n, axis=-1, keepdims=True)
        return base + r_ref[rows, 0:1] * (e - mean_e - n * mean_en)

    for h in range(2):

        def back_two(i, h=h):
            at = pl.multiple_of(h * TOK + i, 32)
            rows = pl.ds(at, 32)
            total = m.own[rows, :] + scatter_sum(m.rbg2, TOK, h, pl.ds(i, 32))
            base = m.cot[pl.ds(pl.multiple_of(b * BLK + at, 32), 32), :].astype(F32)
            g = norm_back(total, 1, m.n2, m.r2, at, base)
            m.gresid[rows, :] = g
            m.gattn[rows, :] = g.astype(BF)

        rows_loop(TOK, 32, back_two, unroll=2)
    poll(2)

    for k, to in ((3, PD), (1, PX), (2, PY)):
        part = dot(m.gattn[...], m.wout[ds(chip(k) * SLP, SLP, SLP), :], 1, 1)
        m.ggs[k - 1] = part[:, :LANES].astype(BF)
        send(f"gg{k}", m.ggs.at[k - 1], m.ggr.at[k, :, low_lanes], to)
        high = part[:, LANES:]
        m.gghs[k - 1] = (high[:TOK] + pltpu.roll(high[TOK:], SL - LANES, 1)).astype(BF)
        send(f"gi{k}", m.gghs.at[k - 1], m.gghr.at[k - 1], to)
    m.ggr[0] = dot(m.gattn[...], m.wout[ds(b * SLP, SLP, SLP), :], 1, 1).astype(BF)
    poll(3)
    for k in range(CHIPS):
        m.tmp[0:SLP, :] = dot(m.grecv[k], m.gattn[...], 0, 0)
        m.goo[k] = m.tmp[ds(c * ROWS, ROWS, 32), :]
        m.gos[k] = m.tmp[ds((1 - c) * ROWS, ROWS, 32), :].astype(BF)
    send("goS", m.gos, m.gor, SIB)
    poll(4)

    gqkv = m.hid
    gres = m.h2
    sent("h2X0", "h2X1", "h2Y0", "h2Y1", "h2F0", "h2F1")

    def mix_back(k):
        j = chip(k)

        def body(i):
            at = pl.multiple_of(j * BLK + i, 16)
            rows = pl.ds(at, 16)
            gg = m.ggr[k, pl.ds(i, 16), :].astype(F32)
            sig = m.sig[rows, :]
            gm = (gg * sig).astype(BF).astype(F32)
            gqkv[rows, 0:SLP] = (
                gg * m.mixed[rows, :].astype(F32) * sig * (1.0 - sig)
            ).astype(BF)
            gnum = gm * m.rden[rows, :]
            gres[rows, 0:SLP] = gnum.astype(BF)
            gres[rows, SLP : 2 * SLP] = (-gnum * m.ratio[rows, :]).astype(BF)

        rows_loop(BLK, 16, body, unroll=2)

    mix_back(0)
    poll(5)
    got("goS")
    for k in (1, 2, 3):
        m.po[k - 1] = (m.goo[k] + m.gor[k].astype(F32)).astype(BF)
    scatter_diagonal("wg", m.po, m.rbo, ROWS // 2)
    scatter_direct_x("wg", m.po, m.rbo, ROWS // 2)
    scatter_direct_y("wg", m.po, m.rbo, ROWS // 2)
    scatter_direct_x("ou", m.pout, m.rbout, TOK)
    scatter_direct_y("ou", m.pout, m.rbout, TOK)
    poll(6)
    for k in (1, 2, 3):
        got(f"gg{k}", f"gi{k}")
        unpack(m.ggr.at[k], m.gghr.at[k - 1])
        mix_back(k)
        poll(6 + k)
    scatter_combine("wg", m.po, m.rbo, ROWS // 2)
    m.sums[...] = dot(ones, gres[:, 0 : 2 * SLP], 1, 0)
    m.gop[...] = jnp.broadcast_to(m.sums[0:1, :], (SEQ, 2 * SLP))
    poll(10)

    def kernel_grad(d):
        return dot(
            gres[ds(d * TOK, TOK, TOK), 0 : 2 * SLP], m.op[pl.ds(band_at(d), BAND), :], 1, 1
        )

    for k in range(CHIPS):
        m.gks[k] = kernel_grad(2 * chip(k) + 1 - c).astype(BF)
    send("gkS", m.gks, m.gkr, SIB)
    poll(11)
    split_rows(m.h1, gqkv.at[:, 0:SLP], m.gqo, m.gqs)
    send("gqS", m.gqs, m.gqr, SIB)
    poll(12)
    for k in range(CHIPS):
        m.gko[k] = kernel_grad(2 * chip(k) + c)
    poll(13)
    got("gkS")
    for k in (1, 2, 3):
        m.pk[k - 1] = (m.gko[k] + m.gkr[k].astype(F32)).astype(BF)
    scatter_diagonal("kg", m.pk, m.rbk, TOK // 2)
    scatter_direct_x("kg", m.pk, m.rbk, TOK // 2)
    scatter_direct_y("kg", m.pk, m.rbk, TOK // 2)
    poll(14)

    def mix_t(d, carry):
        at = pl.ds(band_at(d), BAND)
        m.gop[at, :] += dot(m.kern[d], gres[ds(d * TOK, TOK, TOK), 0 : 2 * SLP], 0, 0)
        return carry

    lax.fori_loop(0, CHIPS * CORES, mix_t, 0)
    poll(15)

    def keys_back(i):
        rows = pl.ds(i, 16)
        gkv = m.gop[rows, 0:SLP]
        w = m.wgt[rows, :]
        gqkv[rows, SLP : 2 * SLP] = (
            (gkv * m.val[rows, :].astype(F32) + m.gop[rows, SLP : 2 * SLP]) * w
        ).astype(BF)
        gqkv[rows, 2 * SLP : 3 * SLP] = (gkv * w).astype(BF)

    rows_loop(SEQ, 16, keys_back, unroll=2)
    poll(16)

    sent("g20", "g21", "g22", "g23", "g24", "g25")
    for k in ORDER:
        part = dot(gqkv[blk_rows(chip(k)), :], m.wqkv[...], 1, 1)
        if k == 0:
            m.own[...] = part
        else:
            m.pgh[k - 1] = part.astype(BF)
        if k == 3:
            scatter_diagonal("g1", m.pgh, m.rbg1, TOK)
        if k == 1:
            scatter_direct_x("g1", m.pgh, m.rbg1, TOK)
        if k == 2:
            scatter_direct_y("g1", m.pgh, m.rbg1, TOK)
        poll(17 + k)
    got("gqS")
    pair_sum_packed("zq", m.gqo, m.gqr, m.zqb)
    poll(21)

    def scattered(dst, mine, came, buf, half):
        for h in range(2):
            rows = pl.ds(h * half, half)
            dst[rows, :] = (
                mine[0, rows, :] + came[0, rows, :].astype(F32)
                + scatter_sum(buf, half, h, pl.ds(0, half))
            ).astype(BF)

    scatter_wait("wg")
    scattered(m.zob, m.goo, m.gor, m.rbo, ROWS // 2)
    z_start("zo")
    poll(22)
    split_rows(m.h1, gqkv.at[:, SLP : 3 * SLP], m.gvo, m.gvs)
    send("gvS", m.gvs, m.gvr, SIB)
    poll(23)
    scatter_combine("kg", m.pk, m.rbk, TOK // 2)
    poll(24)
    scatter_combine("g1", m.pgh, m.rbg1, TOK)
    poll(25)
    got("gvS")
    pair_sum_packed("zv", m.gvo, m.gvr, m.zvb)
    poll(26)
    scatter_combine("ou", m.pout, m.rbout, TOK)
    poll(27)
    poll(28)
    scatter_wait("kg")
    scattered(m.zkb, m.gko, m.gkr, m.rbk, TOK // 2)
    z_start("zk")

    poll(29)

    poll(30)
    scatter_wait("ou")
    for h in range(2):

        def out_rows(i, h=h):
            rows = pl.ds(pl.multiple_of(h * TOK + i, 32), 32)
            m.fout[rows, :] = (
                m.resid[rows, :] + scatter_sum(m.rbout, TOK, h, pl.ds(i, 32))
            ).astype(BF)

        rows_loop(TOK, 32, out_rows)
    send("outS", m.fout.at[other_half], out_out.at[c], SIB)
    local_copy(m.fout.at[own_half], out_out.at[c])

    scatter_wait("g1")
    for h in range(2):

        def back_one(i, h=h):
            at = pl.multiple_of(h * TOK + i, 32)
            rows = pl.ds(at, 32)
            total = m.own[rows, :] + scatter_sum(m.rbg1, TOK, h, pl.ds(i, 32))
            m.fgt[rows, :] = norm_back(total, 0, m.n1, m.r1, at, m.gresid[rows, :]).astype(BF)

        rows_loop(TOK, 32, back_one, unroll=2)
    send("gtS", m.fgt.at[other_half], gtok_out.at[c], SIB)
    local_copy(m.fgt.at[own_half], gtok_out.at[c])
    poll(31)

    for cp in locals_:
        if all(cp is not done for done in (l_tok, l_pb, l_wout, l_wup, l_wdn, l_cot, *l_w)):
            cp.wait()
    for name in begun:
        if name not in in_fetch:
            got(name)
            sent(name)

    @pl.when(fetch)
    def _():
        for name in in_fetch:
            sent(name)

    for name in zitems:
        z_close(name)


FIN_IN = dict(
    gq=((CHIPS, PACK, LANES), BF),
    gv=((CHIPS, 2 * PACK, LANES), BF),
    gup=((CHIPS, ROWS, FS), BF),
    gdn=((FF // (CHIPS * CORES), D), BF),
    gwout=((ROWS, D), BF),
    gpb=((TOK, BAND), BF),
    wq=((ROWS, D), BF),
    wk=((ROWS, D), BF),
    wv=((ROWS, D), BF),
    wup=((ROWS, FF), BF),
    pb=((TOK, BAND), BF),
    out=((2, TOK, D), BF),
    gtok=((2, TOK, D), BF),
)
FIN_OUT = dict(
    q=((ROWS, D), F32),
    k=((ROWS, D), F32),
    v=((ROWS, D), F32),
    o=((ROWS, D), F32),
    up=((ROWS, FF), F32),
    dn=((FF // (CHIPS * CORES), D), F32),
    bias=((TOK, SEQ), F32),
)


def finish_kernel(
    out_in, gtok_in, gq_in, gv_in, gwout_in, gup_in, gdn_in, gpb_in, ga_in, gm_in,
    wq_in, wk_in, wv_in, wup_in, pb_in,
    out_out, gtok_out, ga_out, q_out, k_out, v_out, o_out, gm_out, up_out, dn_out, bias_out,
    *scratch,
):
    m = types.SimpleNamespace(**dict(zip((*FIN_IN, *FIN_OUT), scratch)))
    in_sem, out_sem = scratch[len(FIN_IN) + len(FIN_OUT):]
    start = pl.multiple_of(
        jnp.minimum(jnp.maximum(lax.axis_index("dp") - 2, 0), 3) * LANES, LANES
    )
    stores = []

    def store(src, dst):
        stores.append(pltpu.make_async_copy(src, dst, out_sem.at[len(stores)]))
        stores[-1].start()

    sources = dict(
        gdn=gdn_in, gup=gup_in, wup=wup_in, gq=gq_in, wq=wq_in, gv=gv_in, wk=wk_in, wv=wv_in, gwout=gwout_in,
        gpb=gpb_in, pb=pb_in.at[:, pl.ds(start, BAND)], out=out_in, gtok=gtok_in,
    )
    loads = types.SimpleNamespace(
        **{
            name: pltpu.make_async_copy(src, vars(m)[name], in_sem.at[i])
            for i, (name, src) in enumerate(sources.items())
        }
    )
    for cp in vars(loads).values():
        cp.start()

    loads.gdn.wait()
    m.dn[...] = m.gdn[...].astype(F32)
    store(m.dn, dn_out)

    def as_row(column, gain):
        square = jnp.broadcast_to(column, (ROWS, LANES))
        return jnp.transpose(square)[0:1, :] / gain[...].astype(F32)

    loads.gup.wait()
    loads.wup.wait()
    column = jnp.zeros((ROWS, 1), F32)
    for j in range(CHIPS):
        cols = slice(j * FS, (j + 1) * FS)
        g = m.gup[j].astype(F32)
        m.up[:, cols] = g
        column += jnp.sum(g * m.wup[:, cols].astype(F32), axis=1, keepdims=True)
    store(m.up, up_out)
    gm_out[...] = as_row(column, gm_in)

    def unpack(ref, j, at):
        low = ref[j, at : at + ROWS, :].astype(F32)
        high = ref[j, at + ROWS : at + PACK, :].astype(F32)
        rest = SL - LANES
        return jnp.concatenate(
            [low, jnp.concatenate([high[:, :rest], high[:, rest:]], axis=0)], axis=1
        )

    column = jnp.zeros((ROWS, 1), F32)
    for needs, ref, at, w, mine, dst in (
        ((loads.gq, loads.wq), m.gq, 0, m.wq, m.q, q_out),
        ((loads.gv, loads.wk), m.gv, 0, m.wk, m.k, k_out),
        ((loads.wv,), m.gv, PACK, m.wv, m.v, v_out),
    ):
        for cp in needs:
            cp.wait()
        g = jnp.concatenate([unpack(ref, j, at) for j in range(CHIPS)], axis=1)
        mine[...] = g
        store(mine, dst)
        column += jnp.sum(g * w[...].astype(F32), axis=1, keepdims=True)
    ga_out[...] = as_row(column, ga_in)

    loads.gwout.wait()
    m.o[...] = m.gwout[...].astype(F32)
    store(m.o, o_out)
    loads.gpb.wait()
    loads.pb.wait()
    t_ids = lax.axis_index("dp") * TOK + lax.broadcasted_iota(jnp.int32, (TOK, BAND), 0)
    u_ids = start + lax.broadcasted_iota(jnp.int32, (TOK, BAND), 1)
    m.bias[...] = jnp.zeros((TOK, SEQ), F32)
    m.bias[:, pl.ds(start, BAND)] = jnp.where(
        jnp.abs(t_ids - u_ids) < WIN, m.gpb[...].astype(F32) * jnp.exp(m.pb[...].astype(F32)), 0.0
    )
    store(m.bias, bias_out)
    loads.out.wait()
    store(m.out, out_out)
    loads.gtok.wait()
    store(m.gtok, gtok_out)
    for cp in stores:
        cp.wait()


def plane_program(
    tokens, lengths, cotangent, gain_attn, w_query, w_key, w_value, w_out, gain_mlp, w_up, w_down, pos_bias
):
    anywhere = pl.BlockSpec(memory_space=pl.ANY)
    whole = pl.BlockSpec(memory_space=pltpu.VMEM)
    struct = jax.ShapeDtypeStruct
    results = pl.pallas_call(
        plane_kernel,
        out_shape=(
            struct((2, TOK, D), BF),
            struct((2, TOK, D), BF),
            struct((CHIPS, PACK, LANES), BF),
            struct((CHIPS, 2 * PACK, LANES), BF),
            struct((ROWS, D), BF),
            struct((CHIPS, ROWS, FS), BF),
            struct((CHIPS, ROWS, D), BF),
            struct((TOK, BAND), BF),
        ),
        in_specs=[anywhere, pl.BlockSpec(memory_space=pltpu.SMEM), anywhere, whole, whole] + [anywhere] * 7,
        out_specs=(anywhere,) * 8,
        scratch_shapes=[pltpu.VMEM(shape, kind) for shape, kind in SCRATCH.values()]
        + [
            pltpu.SemaphoreType.DMA((N_REMOTE,)),
            pltpu.SemaphoreType.DMA((N_REMOTE,)),
            pltpu.SemaphoreType.DMA((N_LOCAL,)),
        ],
        compiler_params=pltpu.CompilerParams(
            collective_id=0, has_side_effects=True, vmem_limit_bytes=VMEM_BYTES
        ),
        cost_estimate=pl.CostEstimate(
            flops=15_000_000_000, bytes_accessed=8_000_000, transcendentals=4_000_000
        ),
        name="aft_layer",
    )(
        tokens.reshape(2, TOK, D), lengths.reshape(2), cotangent.reshape(2, TOK, D),
        gain_attn.reshape(1, ROWS), gain_mlp.reshape(1, ROWS),
        w_query, w_key, w_value, w_out, w_up, w_down, pos_bias,
    )
    out, gtok, gq, gv, gwout, gup, gdn, gpb = results
    f32_out = [struct(shape, kind) for shape, kind in FIN_OUT.values()]
    row = struct((1, ROWS), F32)
    out, gtok, grad_gain_a, grad_q, grad_k, grad_v, grad_o, grad_gain_m, grad_up, grad_down, grad_bias = (
        pl.pallas_call(
            finish_kernel,
            out_shape=(struct((2, TOK, D), BF),) * 2 + (row, *f32_out[:4], row, *f32_out[4:]),
            in_specs=[anywhere] * 8 + [whole] * 2 + [anywhere] * 5,
            out_specs=(anywhere, anywhere, whole) + (anywhere,) * 4 + (whole,) + (anywhere,) * 3,
            scratch_shapes=[pltpu.VMEM(shape, kind) for shape, kind in (*FIN_IN.values(), *FIN_OUT.values())]
            + [pltpu.SemaphoreType.DMA((len(FIN_IN),)), pltpu.SemaphoreType.DMA((len(FIN_OUT) + 2,))],
            compiler_params=pltpu.CompilerParams(vmem_limit_bytes=VMEM_BYTES),
            cost_estimate=pl.CostEstimate(flops=4_000_000, bytes_accessed=9_000_000, transcendentals=100_000),
            name="gradients_out",
        )(
            out, gtok, gq, gv, gwout, gup, gdn.reshape(FF // (CHIPS * CORES), D), gpb,
            gain_attn.reshape(1, ROWS), gain_mlp.reshape(1, ROWS),
            w_query, w_key, w_value, w_up, pos_bias,
        )
    )
    return (
        out.reshape(tokens.shape),
        gtok.reshape(tokens.shape),
        grad_gain_a.reshape(ROWS),
        grad_q,
        grad_k,
        grad_v,
        grad_o,
        grad_gain_m.reshape(ROWS),
        grad_up,
        grad_down,
        grad_bias,
    )


def solution(mesh):
    in_specs = (
        P(None, "pipe", "dp", None),
        P(None, "pipe", None),
        P(None, "pipe", "dp", None),
        P("dp"),
        P("dp", None),
        P("dp", None),
        P("dp", None),
        P("dp", None),
        P("dp"),
        P("dp", None),
        P("dp", None),
        P("dp", None),
    )
    out_specs = (
        P(None, "pipe", "dp", None),
        P(None, "pipe", "dp", None),
        P("dp"),
        P("dp", None),
        P("dp", None),
        P("dp", None),
        P("dp", None),
        P("dp"),
        P("dp", None),
        P("dp", None),
        P("dp", None),
    )
    fits = mesh.shape["dp"] == CHIPS * CORES and mesh.shape["pipe"] == DEPTH
    return jax.shard_map(plane_program if fits else local, mesh=mesh, in_specs=in_specs, out_specs=out_specs, check_vma=False)
```

profile of v0, /device:TPU:0, one launch (start us, length us, event | category | flops | bytes accessed | tf_op | source)
XLA Modules:
  0.0 152.1 jit_solution(1508672526628352909)
XLA Ops:
  0.6 146.3 %aft_layer.1 = (bf16[2,128,768]{2,1,0:T(8,128)(2,1)}, bf16[2,128,768]{2,1,0:T(8,128)(2,1)}, bf16[4,144,128]{2,1,0:T(8,128)(2,1)}, bf16[4,288,128]{2,1,0:T(8,128)...) custom-call(bf16[2,128,768]{2,1,0:T(8,128)(2,1)} %bitcast.19, ...), custom_call_target="tpu_custom_call" | custom-call | flops 15000000512 | bytes 8000000 | tf_op jit(solution)/shard_map/aft_layer/pallas_call | solution.py:1439
  146.9 5.0 %gradients_out.1 = (bf16[2,128,768]{2,1,0:T(8,128)(2,1)}, bf16[2,128,768]{2,1,0:T(8,128)(2,1)}, f32[1,96]{1,0:T(1,128)}, f32[96,768]{1,0:T(8,128)}, f32[96,768]{...) custom-call(bf16[2,128,768]{2,1,0:T(8,128)(2,1)} %get-tuple-element., ...), custom_call_target="tpu_custom_call" | custom-call | flops 4000000 | bytes 9000000 | tf_op jit(solution)/shard_map/gradients_out/pallas_call | solution.py:1475
where the time goes:
time: 152 us
  Pallas kernels  151 us (99%)
    pallas_call x1, Pallas kernels, plane_program(): pl.pallas_call(plane_kernel, out_shape=(struct((2, TOK, D), BF), struct((...  146 us
    pallas_call x1, Pallas kernels, plane_program(): pl.pallas_call(finish_kernel, out_shape=(struct((2, TOK, D), BF),) * 2 +...  5.04 us

commit v1 on v0

--- a/solution.py
+++ b/solution.py
@@ -427,8 +427,22 @@
     fgt=((BLK, D), BF),
 )
 POLLS = {
-    1: "d3", 2: "d1", 4: "d2 D3", 6: "d0 D1", 9: "D2", 11: "u3", 13: "D0", 15: "u1", 16: "u2 U3", 23: "u0 U1",
-    25: "U2", 27: "U0", 28: "q3 q1 q2 q0 o", 29: "Q3 v3 Q1 v1 Q2 v2 Q0 v0 O V3 V1 V2 V0 k", 31: "K",
+    1: ("d3",),
+    2: ("d1",),
+    4: ("d2", "D3",),
+    6: ("d0", "D1",),
+    9: ("D2",),
+    11: ("u3",),
+    13: ("D0",),
+    15: ("u1",),
+    16: ("u2",),
+    23: ("u0", "U3",),
+    25: ("U1",),
+    27: ("U2", "U0",),
+    28: ("q3", "q1", "q2", "q0", "o", "+U3", "+U1",),
+    29: ("Q3", "v3", "Q1", "v1", "Q2", "v2", "Q0", "v0", "O", "V3", "V1", "V2", "V0", "k", "+U2", "+U0",),
+    30: ("+Q3", "+Q1", "+Q2", "+Q0",),
+    31: ("K", "+V3", "+V1", "+V2", "+V0", "+O", "+D3", "+D1", "+D2", "+D0", "+K",),
 }
 N_REMOTE = 200
 N_LOCAL = 40
@@ -635,6 +649,9 @@
             total[...] = (base[...].astype(F32) + total[...].astype(F32)).astype(BF)
             back.start()
 
+    def z_take(name):
+        back = zitems[name][5]
+
         @pl.when(outer)
         def _():
             back.wait_recv()
@@ -661,32 +678,35 @@
     z_open("zk", m.zkb, m.zkr, m.zkt)
     ORDER = (3, 1, 2, 0)
 
-    def spread(name, k, total, landing):
-        if k:
-            send(f"{name}{k}", total.at[chip(k)], landing.at[b], peer(k))
-        else:
-            local_copy(total.at[b], landing.at[b])
+    onward = {}
+
+    def prepare(which, k):
+        j = chip(k)
+        whole = dict(D=m.zdt, U=m.zut, Q=m.zqt, V=m.zvt, O=m.zot, K=m.zkt)[which]
+        out = dict(D=gdn_out, U=gup_out, Q=gq_out, V=gv_out, O=gwout_out, K=gpb_out)[which]
+        if which in "UQV" and k:
+            name = f"f{which}{k}"
+            begun.append(name)
+            return make(name, whole.at[j], out.at[b], peer(k))
+        src, dst = (whole, out) if which in "OK" else (whole.at[j], out.at[j])
+        locals_.append(pltpu.make_async_copy(src, dst, local_sem.at[len(locals_)]))
+        return locals_[-1]
 
     def poll(place):
-        for step in POLLS.get(place, "").split():
-            name = "z" + step.lower()
-            if step.islower():
+        for step in POLLS.get(place, ()):
+            code = step.strip("+")
+            name = "z" + code.lower()
+            if code.islower():
                 z_mid(name)
                 continue
-            z_end(name)
-            which, k = step[0], chip(int(step[1:] or 0))
-            if which == "D":
-                local_copy(m.zdt.at[k], gdn_out.at[k])
-            elif which == "U":
-                spread("fu", int(step[1]), m.zut, gup_out)
-            elif which == "Q":
-                spread("fq", int(step[1]), m.zqt, gq_out)
-            elif which == "V":
-                spread("fv", int(step[1]), m.zvt, gv_out)
-            elif which == "O":
-                local_copy(m.zot, gwout_out)
+            if name not in onward:
+                onward[name] = prepare(code[0], int(code[1:] or 0))
+            if step == code:
+                z_end(name)
+                pl.when(inner)(onward[name].start)
             else:
-                local_copy(m.zkt, gpb_out)
+                z_take(name)
+                pl.when(outer)(onward[name].start)
 
     own_half = ds(c * TOK, TOK, TOK)
     other_half = ds((1 - c) * TOK, TOK, TOK)
@@ -1357,8 +1377,8 @@
         stores[-1].start()
 
     sources = dict(
-        gdn=gdn_in, gup=gup_in, wup=wup_in, gq=gq_in, wq=wq_in, gv=gv_in, wk=wk_in, wv=wv_in, gwout=gwout_in,
-        gpb=gpb_in, pb=pb_in.at[:, pl.ds(start, BAND)], out=out_in, gtok=gtok_in,
+        gdn=gdn_in, gup=gup_in, wup=wup_in, out=out_in, gtok=gtok_in, gq=gq_in, wq=wq_in, gv=gv_in, wk=wk_in,
+        wv=wv_in, gwout=gwout_in, gpb=gpb_in, pb=pb_in.at[:, pl.ds(start, BAND)],
     )
     loads = types.SimpleNamespace(
         **{
@@ -1384,8 +1404,12 @@
         cols = slice(j * FS, (j + 1) * FS)
         g = m.gup[j].astype(F32)
         m.up[:, cols] = g
+        store(m.up.at[:, cols], up_out.at[:, cols])
         column += jnp.sum(g * m.wup[:, cols].astype(F32), axis=1, keepdims=True)
-    store(m.up, up_out)
+    loads.out.wait()
+    store(m.out, out_out)
+    loads.gtok.wait()
+    store(m.gtok, gtok_out)
     gm_out[...] = as_row(column, gm_in)
 
     def unpack(ref, j, at):
@@ -1422,10 +1446,6 @@
         jnp.abs(t_ids - u_ids) < WIN, m.gpb[...].astype(F32) * jnp.exp(m.pb[...].astype(F32)), 0.0
     )
     store(m.bias, bias_out)
-    loads.out.wait()
-    store(m.out, out_out)
-    loads.gtok.wait()
-    store(m.gtok, gtok_out)
     for cp in stores:
         cp.wait()
 
@@ -1478,7 +1498,7 @@
             in_specs=[anywhere] * 8 + [whole] * 2 + [anywhere] * 5,
             out_specs=(anywhere, anywhere, whole) + (anywhere,) * 4 + (whole,) + (anywhere,) * 3,
             scratch_shapes=[pltpu.VMEM(shape, kind) for shape, kind in (*FIN_IN.values(), *FIN_OUT.values())]
-            + [pltpu.SemaphoreType.DMA((len(FIN_IN),)), pltpu.SemaphoreType.DMA((len(FIN_OUT) + 2,))],
+            + [pltpu.SemaphoreType.DMA((len(FIN_IN),)), pltpu.SemaphoreType.DMA((len(FIN_OUT) + 1 + CHIPS,))],
             compiler_params=pltpu.CompilerParams(vmem_limit_bytes=VMEM_BYTES),
             cost_estimate=pl.CostEstimate(flops=4_000_000, bytes_accessed=9_000_000, transcendentals=100_000),
             name="gradients_out",

time: 152 us -> 148 us (0.974)
  Pallas kernels: 151 us -> 147 us
    pallas_call x1, Pallas kernels: 146 us -> 142 us  [plane_program(): pl.pallas_call(plane_kernel, out_shape=(struct((2, TOK, D), BF), struct((...]
where the time goes in v1:
time: 148 us
  Pallas kernels  147 us (99%)
    pallas_call x1, Pallas kernels, plane_program(): pl.pallas_call(plane_kernel, out_shape=(struct((2, TOK, D), BF), struct((...  142 us
    pallas_call x1, Pallas kernels, plane_program(): pl.pallas_call(finish_kernel, out_shape=(struct((2, TOK, D), BF),) * 2 +...  4.86 us

profile of v1, /device:TPU:0, one launch (start us, length us, event | category | flops | bytes accessed | tf_op | source)
XLA Modules:
  0.0 147.6 jit_solution(4335609384064566608)
XLA Ops:
  0.6 141.9 %aft_layer.1 = (bf16[2,128,768]{2,1,0:T(8,128)(2,1)}, bf16[2,128,768]{2,1,0:T(8,128)(2,1)}, bf16[4,144,128]{2,1,0:T(8,128)(2,1)}, bf16[4,288,128]{2,1,0:T(8,128)...) custom-call(bf16[2,128,768]{2,1,0:T(8,128)(2,1)} %bitcast.19, ...), custom_call_target="tpu_custom_call" | custom-call | flops 15000000512 | bytes 8000000 | tf_op jit(solution)/shard_map/aft_layer/pallas_call | solution.py:1459
  142.6 4.9 %gradients_out.1 = (bf16[2,128,768]{2,1,0:T(8,128)(2,1)}, bf16[2,128,768]{2,1,0:T(8,128)(2,1)}, f32[1,96]{1,0:T(1,128)}, f32[96,768]{1,0:T(8,128)}, f32[96,768]{...) custom-call(bf16[2,128,768]{2,1,0:T(8,128)(2,1)} %get-tuple-element., ...), custom_call_target="tpu_custom_call" | custom-call | flops 4000000 | bytes 9000000 | tf_op jit(solution)/shard_map/gradients_out/pallas_call | solution.py:1495

commit v2 on v1

--- a/solution.py
+++ b/solution.py
@@ -439,10 +439,10 @@
     23: ("u0", "U3",),
     25: ("U1",),
     27: ("U2", "U0",),
-    28: ("q3", "q1", "q2", "q0", "o", "+U3", "+U1",),
-    29: ("Q3", "v3", "Q1", "v1", "Q2", "v2", "Q0", "v0", "O", "V3", "V1", "V2", "V0", "k", "+U2", "+U0",),
+    28: ("q3", "q1", "q2", "q0", "o0", "o1", "+U3", "+U1",),
+    29: ("Q3", "v3", "Q1", "v1", "Q2", "v2", "Q0", "v0", "O0", "O1", "V3", "V1", "V2", "V0", "k0", "k1", "+U2", "+U0",),
     30: ("+Q3", "+Q1", "+Q2", "+Q0",),
-    31: ("K", "+V3", "+V1", "+V2", "+V0", "+O", "+D3", "+D1", "+D2", "+D0", "+K",),
+    31: ("K0", "K1", "+V3", "+V1", "+V2", "+V0", "+O0", "+O1", "+D3", "+D1", "+D2", "+D0", "+K0", "+K1",),
 }
 N_REMOTE = 200
 N_LOCAL = 40
@@ -614,6 +614,11 @@
 
     zitems = {}
 
+    def half_rows(which, h):
+        size = (ROWS if which == "O" else TOK) // 2
+        return pl.ds(h * size, size)
+
+
     def z_open(name, base, near, total):
         zitems[name] = (
             base,
@@ -674,8 +679,11 @@
         z_open(f"zu{k}", m.zub.at[j], m.zur.at[j], m.zut.at[j])
         z_open(f"zq{k}", m.zqb.at[j], m.zqr.at[j], m.zqt.at[j])
         z_open(f"zv{k}", m.zvb.at[j], m.zvr.at[j], m.zvt.at[j])
-    z_open("zo", m.zob, m.zor, m.zot)
-    z_open("zk", m.zkb, m.zkr, m.zkt)
+    for h in range(2):
+        half = half_rows("O", h)
+        z_open(f"zo{h}", m.zob.at[half], m.zor.at[half], m.zot.at[half])
+        half = half_rows("K", h)
+        z_open(f"zk{h}", m.zkb.at[half], m.zkr.at[half], m.zkt.at[half])
     ORDER = (3, 1, 2, 0)
 
     onward = {}
@@ -688,7 +696,8 @@
             name = f"f{which}{k}"
             begun.append(name)
             return make(name, whole.at[j], out.at[b], peer(k))
-        src, dst = (whole, out) if which in "OK" else (whole.at[j], out.at[j])
+        part = half_rows(which, k) if which in "OK" else j
+        src, dst = whole.at[part], out.at[part]
         locals_.append(pltpu.make_async_copy(src, dst, local_sem.at[len(locals_)]))
         return locals_[-1]
 
@@ -700,7 +709,7 @@
                 z_mid(name)
                 continue
             if name not in onward:
-                onward[name] = prepare(code[0], int(code[1:] or 0))
+                onward[name] = prepare(code[0], int(code[1]))
             if step == code:
                 z_end(name)
                 pl.when(inner)(onward[name].start)
@@ -1028,27 +1037,32 @@
     other_cols = ds((1 - c) * HALF, HALF, LANES)
     own_cols = ds(c * HALF, HALF, LANES)
 
-    def ff_grads(k):
+    def add_product(first, dst, left, right):
+        part = dot(left, right, 0, 0)
+        if first:
+            dst[...] = part
+        else:
+            dst[...] += part
+
+    def down_grads(k):
         rows = blk_rows(chip(k))
-        for dst, at, left, cols, right in (
-            (m.gdx, 0, m.hid, other_cols, m.cot),
-            (m.gdo, 0, m.hid, own_cols, m.cot),
-            (m.guo, 0, m.h2, pl.ds(0, HALF), m.gupr),
-            (m.guo, HALF, m.h2, pl.ds(HALF, HALF), m.gupr),
-        ):
-            part = dot(left[rows, cols], right[rows, :], 0, 0)
-            to = pl.ds(at, HALF)
-            if k == 0:
-                dst[to, :] = part
-            else:
-                dst[to, :] += part
+        add_product(k == 0, m.gdx, m.hid[rows, other_cols], m.cot[rows, :])
+        add_product(k == 0, m.gdo, m.hid[rows, own_cols], m.cot[rows, :])
+
+    def up_grads(k):
+        rows = blk_rows(chip(k))
+        for at in (0, HALF):
+            add_product(
+                k == 0, m.guo.at[pl.ds(at, HALF)], m.h2[rows, at : at + HALF], m.gupr[rows, :]
+            )
 
     ff_forward(0)
     ff_backward(0)
     gather_forward("h2")
     start("ctX1", "ctY0")
     ff_out(0)
-    ff_grads(0)
+    down_grads(0)
+    up_grads(0)
     for k in (1, 2):
         gather_wait("h2", k)
         ff_forward(k)
@@ -1063,17 +1077,12 @@
     gather_wait("ct", 2)
     ff_backward(2)
     scatter_direct_y("g2", m.pgh, m.rbg2, TOK)
-    ff_grads(3)
-    ff_grads(1)
-    scatter_combine("g2", m.pgh, m.rbg2, TOK)
-    ff_grads(2)
+    for k in (3, 1, 2):
+        down_grads(k)
 
     for j in range(CHIPS):
         m.gds[j] = m.gdx[j * ROWS : (j + 1) * ROWS, :].astype(BF)
     send("gdS", m.gds, m.gdr, SIB)
-    for j in range(CHIPS):
-        m.gus[j] = m.guo[ds((2 * j + 1 - c) * ROWS, ROWS, 32), :].astype(BF)
-    send("guS", m.gus, m.gur, SIB)
 
     def split_rows(left, right, kept, leaving):
         width = right.shape[1]
@@ -1104,13 +1113,21 @@
                 pack(base.at[j], i * PACK, total[:, i * SLP : (i + 1) * SLP])
             z_start(f"{name}{k}")
 
+    scatter_combine("g2", m.pgh, m.rbg2, TOK)
+    up_grads(3)
     got("gdS")
     pair_sum("zd", lambda j: m.gdo[ds(j * ROWS, ROWS, 32), :], m.gdr, m.zdb)
+    up_grads(1)
+    up_grads(2)
+    for j in range(CHIPS):
+        m.gus[j] = m.guo[ds((2 * j + 1 - c) * ROWS, ROWS, 32), :].astype(BF)
+    send("guS", m.gus, m.gur, SIB)
+    ff_out(3)
+    scatter_diagonal("ou", m.pout, m.rbout, TOK)
     got("guS")
     pair_sum("zu", lambda j: m.guo[ds((2 * j + c) * ROWS, ROWS, 32), :], m.gur, m.zub)
-    for k in (3, 1, 2):
+    for k in (1, 2):
         ff_out(k)
-    scatter_diagonal("ou", m.pout, m.rbout, TOK)
     poll(1)
 
     scatter_wait("g2")
@@ -1267,7 +1284,8 @@
 
     scatter_wait("wg")
     scattered(m.zob, m.goo, m.gor, m.rbo, ROWS // 2)
-    z_start("zo")
+    z_start("zo0")
+    z_start("zo1")
     poll(22)
     split_rows(m.h1, gqkv.at[:, SLP : 3 * SLP], m.gvo, m.gvs)
     send("gvS", m.gvs, m.gvr, SIB)
@@ -1284,7 +1302,8 @@
     poll(28)
     scatter_wait("kg")
     scattered(m.zkb, m.gko, m.gkr, m.rbk, TOK // 2)
-    z_start("zk")
+    z_start("zk0")
+    z_start("zk1")
 
     poll(29)
 

time: 148 us -> 145 us (0.980)
  Pallas kernels: 147 us -> 144 us
    pallas_call x1, Pallas kernels: 142 us -> 139 us  [plane_program(): pl.pallas_call(plane_kernel, out_shape=(struct((2, TOK, D), BF), struct((...]
where the time goes in v2:
time: 145 us
  Pallas kernels  144 us (99%)
    pallas_call x1, Pallas kernels, plane_program(): pl.pallas_call(plane_kernel, out_shape=(struct((2, TOK, D), BF), struct((...  139 us
    pallas_call x1, Pallas kernels, plane_program(): pl.pallas_call(finish_kernel, out_shape=(struct((2, TOK, D), BF),) * 2 +...  4.86 us

profile of v2, /device:TPU:0, one launch (start us, length us, event | category | flops | bytes accessed | tf_op | source)
XLA Modules:
  0.0 144.6 jit_solution(15379446561961007374)
XLA Ops:
  0.6 138.9 %aft_layer.1 = (bf16[2,128,768]{2,1,0:T(8,128)(2,1)}, bf16[2,128,768]{2,1,0:T(8,128)(2,1)}, bf16[4,144,128]{2,1,0:T(8,128)(2,1)}, bf16[4,288,128]{2,1,0:T(8,128)...) custom-call(bf16[2,128,768]{2,1,0:T(8,128)(2,1)} %bitcast.19, ...), custom_call_target="tpu_custom_call" | custom-call | flops 15000000512 | bytes 8000000 | tf_op jit(solution)/shard_map/aft_layer/pallas_call | solution.py:1478
  139.6 4.9 %gradients_out.1 = (bf16[2,128,768]{2,1,0:T(8,128)(2,1)}, bf16[2,128,768]{2,1,0:T(8,128)(2,1)}, f32[1,96]{1,0:T(1,128)}, f32[96,768]{1,0:T(8,128)}, f32[96,768]{...) custom-call(bf16[2,128,768]{2,1,0:T(8,128)(2,1)} %get-tuple-element., ...), custom_call_target="tpu_custom_call" | custom-call | flops 4000000 | bytes 9000000 | tf_op jit(solution)/shard_map/gradients_out/pallas_call | solution.py:1514

commit v3 on v2

--- a/solution.py
+++ b/solution.py
@@ -1256,6 +1256,8 @@
     rows_loop(SEQ, 16, keys_back, unroll=2)
     poll(16)
 
+    split_rows(m.h1, gqkv.at[:, SLP : 3 * SLP], m.gvo, m.gvs)
+    send("gvS", m.gvs, m.gvr, SIB)
     sent("g20", "g21", "g22", "g23", "g24", "g25")
     for k in ORDER:
         part = dot(gqkv[blk_rows(chip(k)), :], m.wqkv[...], 1, 1)
@@ -1287,8 +1289,6 @@
     z_start("zo0")
     z_start("zo1")
     poll(22)
-    split_rows(m.h1, gqkv.at[:, SLP : 3 * SLP], m.gvo, m.gvs)
-    send("gvS", m.gvs, m.gvr, SIB)
     poll(23)
     scatter_combine("kg", m.pk, m.rbk, TOK // 2)
     poll(24)

time: 145 us -> 146 us (level)
  no operation moved by 1% of the time
where the time goes in v3:
time: 146 us
  Pallas kernels  145 us (99%)
    pallas_call x1, Pallas kernels, plane_program(): pl.pallas_call(plane_kernel, out_shape=(struct((2, TOK, D), BF), struct((...  140 us
    pallas_call x1, Pallas kernels, plane_program(): pl.pallas_call(finish_kernel, out_shape=(struct((2, TOK, D), BF),) * 2 +...  4.86 us

profile of v3, /device:TPU:0, one launch (start us, length us, event | category | flops | bytes accessed | tf_op | source)
XLA Modules:
  0.0 145.8 jit_solution(14543253410530454939)
XLA Ops:
  0.6 140.2 %aft_layer.1 = (bf16[2,128,768]{2,1,0:T(8,128)(2,1)}, bf16[2,128,768]{2,1,0:T(8,128)(2,1)}, bf16[4,144,128]{2,1,0:T(8,128)(2,1)}, bf16[4,288,128]{2,1,0:T(8,128)...) custom-call(bf16[2,128,768]{2,1,0:T(8,128)(2,1)} %bitcast.19, ...), custom_call_target="tpu_custom_call" | custom-call | flops 15000000512 | bytes 8000000 | tf_op jit(solution)/shard_map/aft_layer/pallas_call | solution.py:1478
  140.8 4.9 %gradients_out.1 = (bf16[2,128,768]{2,1,0:T(8,128)(2,1)}, bf16[2,128,768]{2,1,0:T(8,128)(2,1)}, f32[1,96]{1,0:T(1,128)}, f32[96,768]{1,0:T(8,128)}, f32[96,768]{...) custom-call(bf16[2,128,768]{2,1,0:T(8,128)(2,1)} %get-tuple-element., ...), custom_call_target="tpu_custom_call" | custom-call | flops 4000000 | bytes 9000000 | tf_op jit(solution)/shard_map/gradients_out/pallas_call | solution.py:1514
